TPU v7x, 768 devices: a whole 4x8x12 slice. The times are simulated.
768 devices in a mesh: tile: 192 (over z, y_lo, x, core), mode: 4 (over y_hi).
Axes of the slice: x: 4, y: 8 (y_hi: 4, y_lo: 2; y = y_hi * 2 + y_lo), z: 12, core: 2. Of those that a mesh axis runs over, the one named last changes fastest.
Arguments:
- object_field: float32 [2, 24576, 1024], P(None, 'tile'), may hold values from -5 to 5
- components: float32 [4, 4, 2, 128, 128], P('mode'), may hold values from -4 to 4
- relax_weights: float32 [1536, 4], P('tile'), may hold values from -4 to 4
- amplitudes: float32 [1536, 128, 128], P('tile'), may hold values from 0.2 to 4
- positions: int32 [1536, 2], P('tile'), may hold values from 0 to 24575, as said below
- counts: int32 [192], P('tile'), may hold values from 1 to 8, as said below
Outputs:
- object_grad: float32 [2, 24576, 1024], P(None, 'tile', 'mode')
- probe_grad: float32 [4, 4, 2, 128, 128], P('mode')
Inputs may be any that keep to these rules, and one draw needn't show every extreme that they name: positions[j, 0] lies in the rows of the band that holds slot j (128 rows from band index times 128); positions[j, 1] is at most 896; every band has a slot at its last row and one at the last column. `counts`: some band uses all its slots.
All inputs are finite; a program needn't handle non-finite values.
Results may differ from a plain program's by a relative error of at most 0.0003.
Values sent between devices are 32-bit elements; how exact they have to be, the bound alone decides.
A program may use at most 32 MiB of HBM per device.

v0:
```python
import math

import jax
import jax.numpy as jnp
from jax import lax
from jax.sharding import PartitionSpec as P


def passed_along(x, axis, by):
    peers = lax.axis_size(axis)
    pairs = [(i, i + by) for i in range(peers) if 0 <= i + by < peers]
    return lax.ppermute(x, axis, pairs)


def make_tables(patch_size):
    index_line = jnp.arange(patch_size, dtype=jnp.int32)
    product = index_line[:, None] * index_line[None, :] % patch_size
    angle = product.astype(jnp.float32) * (2.0 * math.pi / patch_size)
    scale = 1.0 / math.sqrt(patch_size)
    return (jnp.cos(angle) * scale, -jnp.sin(angle) * scale)


def complex_product(left_part, right_part):
    left_re = left_part[..., 0, :, :]
    left_im = left_part[..., 1, :, :]
    right_re = right_part[..., 0, :, :]
    right_im = right_part[..., 1, :, :]
    return jnp.stack(
        [left_re * right_re - left_im * right_im, left_re * right_im + left_im * right_re], axis=-3
    )


def conjugate(field):
    return jnp.stack([field[..., 0, :, :], -field[..., 1, :, :]], axis=-3)


def transform(field, cos_table, sin_table):
    highest = lax.Precision.HIGHEST
    real_part = field[..., 0, :, :]
    imag_part = field[..., 1, :, :]

    def on_left(matrix, values):
        return jnp.einsum("ab,...bc->...ac", matrix, values, precision=highest)

    def on_right(values, matrix):
        return jnp.einsum("...ab,bc->...ac", values, matrix, precision=highest)

    middle_re = on_left(cos_table, real_part) - on_left(sin_table, imag_part)
    middle_im = on_left(cos_table, imag_part) + on_left(sin_table, real_part)
    out_re = on_right(middle_re, cos_table) - on_right(middle_im, sin_table)
    out_im = on_right(middle_re, sin_table) + on_right(middle_im, cos_table)
    return jnp.stack([out_re, out_im], axis=-3)


def local(object_field, components, relax_weights, amplitudes, positions, counts):
    highest = lax.Precision.HIGHEST
    patch_size = amplitudes.shape[1]
    slot_count = amplitudes.shape[0]
    band_rows = object_field.shape[1]
    cos_table, sin_table = make_tables(patch_size)
    zero_index = jnp.zeros((), jnp.int32)
    below_rows = passed_along(object_field, "tile", -1)
    extended = jnp.concatenate([object_field, below_rows], axis=1)
    first_row = lax.axis_index("tile") * band_rows
    local_rows = positions[:, 0] - first_row
    local_cols = positions[:, 1]
    alive_mask = (jnp.arange(slot_count, dtype=jnp.int32) < counts[0]).astype(jnp.float32)

    def take_patch(row_at, col_at):
        return lax.dynamic_slice(
            extended, (zero_index, row_at, col_at), (2, patch_size, patch_size)
        )

    patches = jax.vmap(take_patch)(local_rows, local_cols)
    probes = jnp.einsum("sc,kcxyz->skxyz", relax_weights, components, precision=highest)
    far_field = transform(complex_product(probes, patches[:, None]), cos_table, sin_table)
    local_power = jnp.sum(far_field * far_field, axis=(1, 2))
    intensity = lax.psum(local_power, "mode")
    factor = alive_mask[:, None, None] * (1.0 - amplitudes / jnp.sqrt(jnp.maximum(intensity, 1.0)))
    residue = far_field * factor[:, None, None]
    back_waves = transform(residue, cos_table, -sin_table)
    patch_grad = jnp.sum(complex_product(conjugate(probes), back_waves), axis=1)

    def place_patch(index_slot, grad_field):
        row_at = local_rows[index_slot]
        col_at = local_cols[index_slot]
        current = lax.dynamic_slice(
            grad_field, (zero_index, row_at, col_at), (2, patch_size, patch_size)
        )
        return lax.dynamic_update_slice(
            grad_field, current + patch_grad[index_slot], (zero_index, row_at, col_at)
        )

    grad_extended = lax.fori_loop(0, slot_count, place_patch, jnp.zeros_like(extended))
    probe_terms = complex_product(conjugate(patches)[:, None], back_waves)
    local_probe = jnp.einsum("sc,skxyz->kcxyz", relax_weights, probe_terms, precision=highest)
    probe_grad = lax.psum(local_probe, "tile")
    rim_in = passed_along(grad_extended[:, band_rows:, :], "tile", 1)
    whole_grad = grad_extended[:, :band_rows, :].at[:, :patch_size, :].add(rim_in)
    object_grad = lax.psum_scatter(whole_grad, "mode", scatter_dimension=2, tiled=True)
    return (object_grad, probe_grad)


def solution(mesh):
    return jax.shard_map(
        local,
        mesh=mesh,
        in_specs=(
            P(None, "tile", None),
            P("mode", None, None, None, None),
            P("tile", None),
            P("tile", None, None),
            P("tile", None),
            P("tile"),
        ),
        out_specs=(P(None, "tile", "mode"), P("mode", None, None, None, None)),
        check_vma=False,
    )
```

profile of v0, /device:TPU:1, one launch (start us, length us, event | category | flops | bytes accessed | tf_op | source)
XLA Modules:
  0.0 1771.5 jit_solution(2925088131683551368)
XLA Ops:
  7.2 12.6 collective-permute-start
  20.6 2.2 convolution_bitcast_fusion
  22.8 1.9 collective-permute-done
  24.7 2.8 pad_maximum_fusion
  27.4 61.7 %while.17 = (s32[]{:T(128)}, f32[2,256,1024]{2,1,0:T(8,128)}, s32[8,3]{0,1:T(4,128)S(1)}, f32[8,2,128,128]{3,0,2,1:T(8,128)}, s32[]{:T(128)}, /*index=5*/s32[]{:T(128)}) while((s32[]{:T(128)}, f32[2,256,1024]{2,1,0:T(8,128)}, s32[8,3]{0,1:T(4,128)S(1)}, f32[8,2,128,128]{3,0,2,1:T(8,128)}, s32[]{:T(128)}, /*index=5*/s32[]{:T(128)}) %tuple.64), condition=%wide.while_cond.1, body=%wide.while_body.1.sunk | while | flops 2 | bytes 524421 | solution.py:70
  28.0 2.3 constant_dynamic-slice_fusion.8
  30.4 4.8 dynamic-update-slice.5
  35.7 2.3 constant_dynamic-slice_fusion.8
  38.1 4.8 dynamic-update-slice.5
  43.5 2.3 constant_dynamic-slice_fusion.8
  45.8 4.8 dynamic-update-slice.5
  51.2 2.3 constant_dynamic-slice_fusion.8
  53.5 4.8 dynamic-update-slice.5
  58.9 2.3 constant_dynamic-slice_fusion.8
  61.2 4.8 dynamic-update-slice.5
  66.6 2.3 constant_dynamic-slice_fusion.8
  68.9 4.8 dynamic-update-slice.5
  74.3 2.3 constant_dynamic-slice_fusion.8
  76.6 4.8 dynamic-update-slice.5
  82.0 2.3 constant_dynamic-slice_fusion.8
  84.3 4.8 dynamic-update-slice.5
  102.9 69.7 %all-reduce.3.cloned.1.call-done = f32[8,128,128]{2,1,0:T(8,128)} async-done(((f32[8,128,128]{2,1,0:T(8,128)}), f32[8,128,128]{2,1,0:T(8,128)}) %all-reduce.3.cloned.1.call-update) | async-done | bytes 524304 | tf_op jit(solution)/shard_map/psum | solution.py:78
  175.1 1.9 fusion.11
  178.1 1.9 fusion.1
  181.4 1.6 fusion.15
  183.0 1.6 fusion.27
  184.6 1.9 fusion
  188.7 3.2 subtract_bitcast_fusion
  193.1 65.5 %while.16 = (s32[]{:T(128)}, f32[2,256,1024]{2,1,0:T(8,128)S(1)}, s32[8]{0:T(128)S(1)}, s32[8]{0:T(128)S(1)}, f32[8,2,128,128]{3,0,2,1:T(8,128)}, /*index=5*/s32[]{:T(128)}, s32[]{:T(128)}, s32[]{:T(128)}, s32[]{:T(128)}) while((s32[]{:T(128)}, f32[2,256,1024]{2,1,0:T(8,128)S(1)}, s32[8]{0:T(128)S(1)}, s32[8]{0:T(128)S(1)}, ...), condition=%wide.region_3.4_spmd, body=%wide.region_2.3_spmd.sunk | while | flops 32776 | bytes 917713 | solution.py:94
  197.7 1.3 constant_dynamic-slice_fusion.6
  199.1 2.5 dynamic_update_slice.8
  207.7 2.1 dynamic_update_slice.8
  214.4 1.3 constant_dynamic-slice_fusion.6
  215.9 2.1 dynamic_update_slice.8
  222.6 1.3 constant_dynamic-slice_fusion.6
  224.1 2.5 dynamic_update_slice.8
  232.6 2.1 dynamic_update_slice.8
  239.3 1.3 constant_dynamic-slice_fusion.6
  246.4 1.3 constant_dynamic-slice_fusion.6
  247.8 2.5 dynamic_update_slice.8
  256.3 2.3 dynamic_update_slice.8
  259.7 4.0 collective-permute-start.1
  263.8 1.8 convolution_bitcast_fusion.1
  265.6 10.2 collective-permute-done.1
  275.8 2.4 slice_add_fusion
  278.2 1445.7 %all-reduce.5.cloned.1.call-done = f32[1,4,2,128,128]{4,1,3,2,0:T(4,128)} async-done(((f32[1,4,2,128,128]{4,1,3,2,0:T(4,128)}), f32[1,4,2,128,128]{4,1,3,2,0:T(4,128)}) %all-reduce.5.cloned.1.call-update) | async-done | bytes 524304 | tf_op jit(solution)/shard_map/psum | solution.py:97
  1723.9 1.9 copy.33
  1725.8 39.2 %reduce-scatter.2.cloned.1.call-done = f32[2,128,256]{2,1,0:T(8,128)} async-done(((f32[2,128,1024]{2,1,0:T(8,128)}), f32[2,128,256]{2,1,0:T(8,128)}) %reduce-scatter.2.cloned.1.call-update) | async-done | bytes 262160 | tf_op jit(solution)/shard_map/reduce_scatter | solution.py:100
  (92 shorter events, 43.3 us)
Async XLA Ops:
  7.2 13.4 copy-start
  7.2 17.5 copy-start.5
  7.2 165.5 %all-reduce.3.cloned.1.call-start = ((), (), s32[]{:S(2)}) async-start(), calls=%async_computation.1 | async-start | bytes 1048576 | tf_op jit(solution)/shard_map/psum | solution.py:78
  7.2 17.4 collective-permute-start
  98.7 73.9 %copy-start.1 = (f32[8,1,1,128,128]{4,3,0,2,1:T(8,128)}, f32[8,1,1,128,128]{4,3,0,2,1:T(8,128)S(1)}, u32[]{:S(2)}) copy-start(f32[8,1,1,128,128]{4,3,0,2,1:T(8,128)S(1)} %fusion.3) | copy-start | bytes 1572868
  99.7 1624.1 %all-reduce.5.cloned.1.call-start = ((), (), s32[]{:S(2)}) async-start(), calls=%async_computation.3 | async-start | bytes 1048576 | tf_op jit(solution)/shard_map/psum | solution.py:97
  181.3 3.3 copy-start.3
  184.6 3.2 copy-start.4
  258.6 5.1 copy-start.2
  258.6 5.1 copy-start.6
  259.7 16.1 collective-permute-start.1
  265.6 1499.4 %reduce-scatter.2.cloned.1.call-start = ((), (), s32[]{:S(2)}) async-start(), calls=%async_computation.2 | async-start | bytes 1310720 | tf_op jit(solution)/shard_map/reduce_scatter | solution.py:100
Sparse Core Ops, SparseCore 0:
  99.9 72.7 all-reduce.2
  265.7 1458.1 all-reduce.4
  1727.9 37.0 reduce-scatter.1
where the time goes:
time: 1770 us
  waiting for transfers between devices  1570 us (89%)
  local copies, waits for them, and re-layouts  105 us (6%)
  loops' own time  27.6 us (2%)
  matrix products  25.9 us (1%)
    psum x1, waiting for transfers between devices, local(): probe_grad = lax.psum(local_probe, 'tile')  1450 us
    psum x1, waiting for transfers between devices, local(): intensity = lax.psum(local_power, 'mode')  69.7 us
    gather x32, local copies, waits for them, and re-layouts  61.6 us
    reduce_scatter x1, waiting for transfers between devices, local(): lax.psum_scatter(whole_grad, 'mode', scatter_dimension=2, tiled=True)  39.2 us
  transfers between devices with their start and end apart: 5, of which 5 were waited for; matrix products, arithmetic and copies ran while one was open for 1% of the time, Pallas kernels for 0%

commit v1 on v0

v1 whole, which is shorter than its diff:
```python
import functools
import math

import jax
import jax.numpy as jnp
import numpy as np
from jax import lax
from jax.experimental import pallas as pl
from jax.experimental.pallas import tpu as pltpu
from jax.sharding import PartitionSpec as P

MESH = pl.DeviceIdType.MESH
SIDE = 128
SLOTS = 8
COMP = 4
MODES = 4
TILES_WIDE = 8
QUARTER = 32
HALF = 16
EMPTY = 2 * SLOTS


def group_size(tiles):
    return 16 if tiles % 16 == 0 else 2


def owner_count(depth):
    return 1 << (depth.bit_length() - 1)


def split(values):
    high = values.astype(jnp.bfloat16)
    low = (values - high.astype(jnp.float32)).astype(jnp.bfloat16)
    return high, low


def dot(left, right):
    return jnp.dot(left, right, preferred_element_type=jnp.float32)


def both_sides(wide, right_high, right_low, left_high, left_low):
    high, low = split(wide)
    middle = dot(high, right_high) + dot(low, right_high) + dot(high, right_low)
    tall = jnp.concatenate([middle[:, :SIDE], middle[:, SIDE:]], axis=0)
    high, low = split(tall)
    return dot(left_high, high) + dot(left_high, low) + dot(left_low, high)


def kernel(
    tiles,
    object_ref,
    components_ref,
    weights_ref,
    amplitudes_ref,
    positions_ref,
    counts_ref,
    row_high,
    row_low,
    col_high,
    col_low,
    object_out,
    probe_out,
    ext,
    comp,
    amps,
    patches,
    probes,
    far,
    power,
    pair_in,
    pair_mid,
    pair_sum,
    factor,
    placed,
    rim_out,
    rim_in,
    part,
    part_in,
    terms,
    chunk,
    near_buf,
    far_buf,
    local_sems,
    halo_sems,
    slot_sems,
    rim_sems,
    part_sems,
    near_sems,
    far_sems,
    back_sems,
    spread_sems,
):
    group = group_size(tiles)
    depth = tiles // group
    owners = owner_count(depth)
    rows = COMP * 2 * SIDE // group
    piece = rows // owners
    tile = lax.axis_index("tile")
    mode = lax.axis_index("mode")
    above = lax.rem(tile + tiles - 1, tiles)
    below = lax.rem(tile + 1, tiles)
    right = lax.rem(mode + 1, MODES)
    left = lax.rem(mode + MODES - 1, MODES)
    mine = lax.rem(tile, group)
    level = lax.div(tile, group)

    def near(step):
        return level * group + lax.rem(mine + step, group)

    def beyond(step):
        return lax.rem(level + step, depth) * group + mine

    def send(src, dst, sems, peer):
        return pltpu.make_async_remote_copy(
            src_ref=src,
            dst_ref=dst,
            send_sem=sems.at[0],
            recv_sem=sems.at[1],
            device_id=peer,
            device_id_type=MESH,
        )

    def columns(ref, at):
        return ref.at[:, :, pl.ds(at * SIDE, SIDE)]

    loads = [
        pltpu.make_async_copy(components_ref.at[0], comp, local_sems.at[0]),
        pltpu.make_async_copy(
            amplitudes_ref.at[:, pl.ds(pl.multiple_of(mode * QUARTER, 8), QUARTER), :],
            amps,
            local_sems.at[1],
        ),
    ] + [
        pltpu.make_async_copy(
            columns(object_ref, at), ext.at[:, at, pl.ds(0, SIDE), :], local_sems.at[2 + at]
        )
        for at in range(TILES_WIDE)
    ]
    for copy in loads:
        copy.start()

    barrier = pltpu.get_barrier_semaphore()
    peers = [{"tile": above}, {"tile": below}, {"mode": right}, {"mode": left}]
    peers += [{"tile": near(step)} for step in range(1, group)]
    peers += [{"tile": beyond(step)} for step in range(1, depth)]
    for peer in peers:
        pl.semaphore_signal(barrier, inc=1, device_id=peer, device_id_type=MESH)
    pl.semaphore_wait(barrier, len(peers))

    halo = [
        send(
            columns(object_ref, at),
            ext.at[:, at, pl.ds(SIDE, SIDE), :],
            halo_sems.at[:, at],
            {"tile": above},
        )
        for at in range(TILES_WIDE)
    ]
    for copy in halo:
        copy.start()

    terms[...] = jnp.zeros_like(terms)

    def clear(at, carry):
        for plane in range(2):
            placed[plane, at, pl.ds(0, SIDE), :] = jnp.zeros((SIDE, SIDE), jnp.float32)
            placed[plane, at, pl.ds(2 * SIDE, SIDE), :] = jnp.zeros((SIDE, SIDE), jnp.float32)
        return carry

    lax.fori_loop(0, EMPTY + 1, clear, 0)
    for plane in range(2):
        placed[plane, EMPTY, pl.ds(SIDE, SIDE), :] = jnp.zeros((SIDE, SIDE), jnp.float32)
    for copy in loads:
        copy.wait()

    def mix(slot, carry):
        for plane in range(2):
            total = weights_ref[slot, 0] * comp[0, plane]
            for at in range(1, COMP):
                total = total + weights_ref[slot, at] * comp[at, plane]
            probes[slot, plane] = total
        return carry

    lax.fori_loop(0, SLOTS, mix, 0)
    for copy in halo:
        copy.wait_recv()

    @pl.when(tile == tiles - 1)
    def _():
        for plane in range(2):
            for at in range(TILES_WIDE):
                ext[plane, at, pl.ds(SIDE, SIDE), :] = jnp.zeros((SIDE, SIDE), jnp.float32)

    lane = lax.broadcasted_iota(jnp.int32, (SIDE, SIDE), 1)

    def place_of(slot):
        row = positions_ref[slot, 0] & (SIDE - 1)
        col = positions_ref[slot, 1]
        base = jnp.minimum(lax.shift_right_logical(col, 7), TILES_WIDE - 2)
        return row, base, col - base * SIDE

    def take(slot, plane):
        row, base, shift = place_of(slot)
        turn = (SIDE - shift) & (SIDE - 1)
        first = pltpu.roll(ext[plane, base, pl.ds(row, SIDE), :], turn, 1)
        second = pltpu.roll(ext[plane, base + 1, pl.ds(row, SIDE), :], turn, 1)
        return jnp.where(lane < SIDE - shift, first, second)

    ahead = pl.multiple_of(lax.rem(QUARTER * (mode + 1) + HALF, SIDE), 8)
    behind = pl.multiple_of(lax.rem(QUARTER * (mode + 2) + HALF, SIDE), 8)
    own_rows = pl.multiple_of(QUARTER * mode, 8)
    right_rows = pl.multiple_of(QUARTER * right, 8)
    left_rows = pl.multiple_of(QUARTER * left, 8)

    def first_pass(slot):
        return [
            send(
                power.at[slot, pl.ds(ahead, QUARTER), :],
                pair_in.at[slot, 0],
                slot_sems.at[:, slot, 0],
                {"mode": right},
            ),
            send(
                power.at[slot, pl.ds(behind, QUARTER), :],
                pair_in.at[slot, 1],
                slot_sems.at[:, slot, 1],
                {"mode": left},
            ),
        ]

    def second_pass(slot):
        return [
            send(
                pair_mid.at[slot, 0],
                pair_sum.at[slot, 0],
                slot_sems.at[:, slot, 2],
                {"mode": right},
            ),
            send(
                pair_mid.at[slot, 1],
                pair_sum.at[slot, 1],
                slot_sems.at[:, slot, 3],
                {"mode": left},
            ),
        ]

    def factor_rows(slot, start, count):
        return factor.at[slot, pl.ds(start, count), :]

    def third_pass(slot):
        mid = factor_rows(slot, own_rows, QUARTER)
        return [
            send(mid, mid, slot_sems.at[:, slot, 4], {"mode": right}),
            send(mid, mid, slot_sems.at[:, slot, 5], {"mode": left}),
        ]

    def fourth_pass(slot):
        top = factor_rows(slot, left_rows, HALF)
        bottom = factor_rows(slot, pl.multiple_of(right_rows + HALF, 8), HALF)
        return [
            send(top, top, slot_sems.at[:, slot, 6], {"mode": right}),
            send(bottom, bottom, slot_sems.at[:, slot, 7], {"mode": left}),
        ]

    def forward(slot):
        for plane in range(2):
            patches[slot, plane] = take(slot, plane)
        probe_re, probe_im = probes[slot, 0], probes[slot, 1]
        patch_re, patch_im = patches[slot, 0], patches[slot, 1]
        wide = jnp.concatenate(
            [
                probe_re * patch_re - probe_im * patch_im,
                probe_re * patch_im + probe_im * patch_re,
            ],
            axis=1,
        )
        wave = both_sides(wide, row_high[...], row_low[...], col_high[...], col_low[...])
        far[slot] = wave
        strength = wave[:SIDE] * wave[:SIDE] + wave[SIDE:] * wave[SIDE:]
        power[slot, pl.ds(0, SIDE), :] = strength
        power[slot, pl.ds(SIDE, HALF), :] = strength[:HALF]
        for copy in first_pass(slot):
            copy.start()

    def relay_power(slot):
        to_right, to_left = first_pass(slot)
        go_right, go_left = second_pass(slot)
        to_right.wait_recv()
        pair_mid[slot, 0] = pair_in[slot, 0, pl.ds(HALF, HALF), :] + power[slot, pl.ds(right_rows, HALF), :]
        go_right.start()
        to_left.wait_recv()
        pair_mid[slot, 1] = (
            pair_in[slot, 1, pl.ds(0, HALF), :]
            + power[slot, pl.ds(pl.multiple_of(left_rows + HALF, 8), HALF), :]
        )
        go_left.start()

    def make_factor(slot):
        for copy in second_pass(slot):
            copy.wait_recv()
        own = power[slot, pl.ds(own_rows, QUARTER), :]
        top = own[:HALF] + pair_sum[slot, 0] + pair_in[slot, 1, pl.ds(HALF, HALF), :]
        bottom = own[HALF:] + pair_sum[slot, 1] + pair_in[slot, 0, pl.ds(0, HALF), :]
        intensity = jnp.concatenate([top, bottom], axis=0)
        ratio = 1.0 - amps[slot] * lax.rsqrt(jnp.maximum(intensity, 1.0))
        factor[slot, pl.ds(own_rows, QUARTER), :] = jnp.where(slot < counts_ref[0], ratio, 0.0)
        for copy in third_pass(slot):
            copy.start()

    def relay_factor(slot):
        go_right, go_left = fourth_pass(slot)
        from_left = factor_rows(slot, left_rows, QUARTER)
        send(from_left, from_left, slot_sems.at[:, slot, 4], {"mode": right}).wait_recv()
        go_right.start()
        from_right = factor_rows(slot, right_rows, QUARTER)
        send(from_right, from_right, slot_sems.at[:, slot, 5], {"mode": left}).wait_recv()
        go_left.start()

    def backward(slot):
        across = pl.multiple_of(QUARTER * lax.rem(mode + 2, MODES), 8)
        top = factor_rows(slot, across, HALF)
        send(top, top, slot_sems.at[:, slot, 6], {"mode": right}).wait_recv()
        bottom = factor_rows(slot, pl.multiple_of(across + HALF, 8), HALF)
        send(bottom, bottom, slot_sems.at[:, slot, 7], {"mode": left}).wait_recv()
        scale = factor[slot]
        wave = far[slot]
        wide = jnp.concatenate([wave[:SIDE] * scale, wave[SIDE:] * scale], axis=1)
        back = both_sides(wide, col_high[...], col_low[...], row_high[...], row_low[...])
        back_re, back_im = back[:SIDE], back[SIDE:]
        probe_re, probe_im = probes[slot, 0], probes[slot, 1]
        shift = place_of(slot)[2]
        grads = (
            probe_re * back_re + probe_im * back_im,
            probe_re * back_im - probe_im * back_re,
        )
        for plane in range(2):
            turned = pltpu.roll(grads[plane], shift & (SIDE - 1), 1)
            placed[plane, 2 * slot, pl.ds(SIDE, SIDE), :] = jnp.where(lane >= shift, turned, 0.0)
            placed[plane, 2 * slot + 1, pl.ds(SIDE, SIDE), :] = jnp.where(lane < shift, turned, 0.0)
        patch_re, patch_im = patches[slot, 0], patches[slot, 1]
        pieces = (
            patch_re * back_re + patch_im * back_im,
            patch_re * back_im - patch_im * back_re,
        )
        for at in range(COMP):
            for plane in range(2):
                where_at = pl.ds((2 * at + plane) * SIDE, SIDE)
                terms[where_at, :] = terms[where_at, :] + weights_ref[slot, at] * pieces[plane]

    stages = (forward, relay_power, make_factor, relay_factor, backward)

    def step(at, carry):
        for lag, stage in enumerate(stages):

            @pl.when((at >= lag) & (at < SLOTS + lag))
            def _():
                stage(at - lag)

        return carry

    lax.fori_loop(0, SLOTS + len(stages) - 1, step, 0)

    def gathered(plane, tile_at, start):
        total = None
        for slot in range(SLOTS):
            row, base, shift = place_of(slot)
            index = jnp.where(
                tile_at == base, 2 * slot, jnp.where(tile_at == base + 1, 2 * slot + 1, EMPTY)
            )
            value = placed[plane, index, pl.ds(start - row, SIDE), :]
            total = value if total is None else total + value
        return total

    order = ((2, 0), (2, 1), (1, 1), (3, 0), (1, 0), (3, 1), (0, 0), (0, 1))

    def block_of(at):
        turn, plane = order[at]
        return lax.rem(mode + turn, MODES), plane

    rims = []
    for at in range(8):
        block, plane = block_of(at)
        for half in range(2):
            rim_out[at, half] = gathered(plane, 2 * block + half, 2 * SIDE)
        copy = send(rim_out.at[at], rim_in.at[at], rim_sems.at[:, at], {"tile": below})
        copy.start()
        rims.append(copy)

    def chunk_rows(at):
        return pl.ds(pl.multiple_of(at * rows, 8), rows)

    spread = [
        send(
            terms.at[chunk_rows(lax.rem(mine + step, group))],
            near_buf.at[step],
            near_sems.at[:, step],
            {"tile": near(step)},
        )
        for step in range(1, group)
    ]
    for copy in spread:
        copy.start()

    part_peers = ({"mode": right}, {"mode": left})
    part_kind = (0, 2, 1, 3, 4, 5)
    part_side = (0, 1, 0, 1, 0, 1)
    parts = [
        send(
            part.at[at],
            part_in.at[part_kind[at]],
            part_sems.at[:, part_kind[at]],
            part_peers[part_side[at]],
        )
        for at in range(6)
    ]
    arrivals = {part_kind[at]: parts[at] for at in range(6)}

    def whole(at, extra):
        block, plane = block_of(at)
        rims[at].wait_recv()
        for kind in extra:
            arrivals[kind].wait_recv()
        for half in range(2):
            value = gathered(plane, 2 * block + half, SIDE)
            value = value + jnp.where(tile > 0, rim_in[at, half], 0.0)
            for kind in extra:
                value = value + part_in[kind, half]
            yield half, value

    for at in range(4):
        for half, value in whole(at, ()):
            part[at, half] = value
        parts[at].start()

    for copy in spread:
        copy.wait_recv()
    total = terms[chunk_rows(mine), :]
    for step in range(1, group):
        total = total + near_buf[step]
    chunk[...] = total

    def to_owner(step):
        target = lax.rem(level + step, depth)
        at = pl.ds(pl.multiple_of(lax.rem(target, owners) * piece, 8), piece)
        return target, send(
            chunk.at[at], far_buf.at[step], far_sems.at[:, step], {"tile": beyond(step)}
        )

    def from_owner(source, step):
        at = pl.ds(pl.multiple_of(mine * rows + lax.rem(source, owners) * piece, 8), piece)
        return send(
            probe_out.at[at], probe_out.at[at], back_sems.at[:, step], {"tile": beyond(step)}
        )

    for step in range(1, depth):
        target, copy = to_owner(step)

        @pl.when(target < owners)
        def _():
            copy.start()

    for at in range(4, 6):
        for half, value in whole(at, (2 * (at - 4),)):
            part[at, half] = value
        parts[at].start()

    @pl.when(level < owners)
    def _():
        for step in range(1, depth):
            to_owner(step)[1].wait_recv()
        total = chunk[pl.ds(pl.multiple_of(lax.rem(level, owners) * piece, 8), piece), :]
        for step in range(1, depth):
            total = total + far_buf[step]
        at = pl.ds(pl.multiple_of(mine * rows + lax.rem(level, owners) * piece, 8), piece)
        probe_out[at, :] = total
        for step in range(1, depth):
            from_owner(level, step).start()

    for step in range(1, depth):
        source = lax.rem(level - step + depth, depth)

        @pl.when(source < owners)
        def _():
            from_owner(source, step).wait_recv()

    def shared(source, step):
        at = chunk_rows(source)
        return send(
            probe_out.at[at], probe_out.at[at], spread_sems.at[:, step], {"tile": near(step)}
        )

    for step in range(1, group):
        shared(mine, step).start()

    for at in range(6, 8):
        for half, value in whole(at, (4, 3) if at == 6 else (5, 1)):
            object_out[at - 6, :, pl.ds(half * SIDE, SIDE)] = value

    for step in range(1, group):
        shared(lax.rem(mine - step + group, group), step).wait_recv()

    for copy in halo + rims + parts + spread:
        copy.wait_send()
    for step in range(1, group):
        shared(mine, step).wait_send()
    for step in range(1, depth):
        target, copy = to_owner(step)

        @pl.when(target < owners)
        def _():
            copy.wait_send()

    @pl.when(level < owners)
    def _():
        for step in range(1, depth):
            from_owner(level, step).wait_send()

    def settle(slot, carry):
        for make in (first_pass, second_pass, third_pass, fourth_pass):
            for copy in make(slot):
                copy.wait_send()
        return carry

    lax.fori_loop(0, SLOTS, settle, 0)


def tables():
    line = np.arange(SIDE)
    angle = (line[:, None] * line[None, :] % SIDE) * (2.0 * math.pi / SIDE)
    cos = np.cos(angle) / math.sqrt(SIDE)
    sin = -np.sin(angle) / math.sqrt(SIDE)
    row = np.block([[cos, sin], [-sin, cos]])
    kinds = []
    for full in (row, row.T):
        high = full.astype(np.float32).astype(jnp.bfloat16)
        low = (full - high.astype(np.float64)).astype(np.float32).astype(jnp.bfloat16)
        kinds += [high, low]
    return kinds


def local(object_field, components, relax_weights, amplitudes, positions, counts):
    tiles = lax.axis_size("tile")
    group = group_size(tiles)
    depth = tiles // group
    rows = COMP * 2 * SIDE // group
    piece = rows // owner_count(depth)
    f32 = jnp.float32
    anywhere = pl.BlockSpec(memory_space=pl.ANY)
    scalars = pl.BlockSpec(memory_space=pltpu.SMEM)
    vector = pl.BlockSpec(memory_space=pltpu.VMEM)
    flops = 2 * 2 * SLOTS * 3 * 2 * 256 * 256 * 128
    object_grad, probe_grad = pl.pallas_call(
        functools.partial(kernel, tiles),
        out_shape=(
            jax.ShapeDtypeStruct((2, SIDE, 2 * SIDE), f32),
            jax.ShapeDtypeStruct((COMP * 2 * SIDE, SIDE), f32),
        ),
        in_specs=[anywhere, anywhere, scalars, anywhere, scalars, scalars] + [vector] * 4,
        out_specs=(vector, vector),
        scratch_shapes=[
            pltpu.VMEM((2, TILES_WIDE, 2 * SIDE, SIDE), f32),
            pltpu.VMEM((COMP, 2, SIDE, SIDE), f32),
            pltpu.VMEM((SLOTS, QUARTER, SIDE), f32),
            pltpu.VMEM((SLOTS, 2, SIDE, SIDE), f32),
            pltpu.VMEM((SLOTS, 2, SIDE, SIDE), f32),
            pltpu.VMEM((SLOTS, 2 * SIDE, SIDE), f32),
            pltpu.VMEM((SLOTS, SIDE + HALF, SIDE), f32),
            pltpu.VMEM((SLOTS, 2, QUARTER, SIDE), f32),
            pltpu.VMEM((SLOTS, 2, HALF, SIDE), f32),
            pltpu.VMEM((SLOTS, 2, HALF, SIDE), f32),
            pltpu.VMEM((SLOTS, SIDE, SIDE), f32),
            pltpu.VMEM((2, EMPTY + 1, 3 * SIDE, SIDE), f32),
            pltpu.VMEM((8, 2, SIDE, SIDE), f32),
            pltpu.VMEM((8, 2, SIDE, SIDE), f32),
            pltpu.VMEM((6, 2, SIDE, SIDE), f32),
            pltpu.VMEM((6, 2, SIDE, SIDE), f32),
            pltpu.VMEM((COMP * 2 * SIDE, SIDE), f32),
            pltpu.VMEM((rows, SIDE), f32),
            pltpu.VMEM((group, rows, SIDE), f32),
            pltpu.VMEM((depth, piece, SIDE), f32),
            pltpu.SemaphoreType.DMA((2 + TILES_WIDE,)),
            pltpu.SemaphoreType.DMA((2, TILES_WIDE)),
            pltpu.SemaphoreType.DMA((2, SLOTS, 8)),
            pltpu.SemaphoreType.DMA((2, 8)),
            pltpu.SemaphoreType.DMA((2, 6)),
            pltpu.SemaphoreType.DMA((2, group)),
            pltpu.SemaphoreType.DMA((2, depth)),
            pltpu.SemaphoreType.DMA((2, depth)),
            pltpu.SemaphoreType.DMA((2, group)),
        ],
        compiler_params=pltpu.CompilerParams(
            collective_id=0, has_side_effects=True, vmem_limit_bytes=48 * 1024 * 1024
        ),
        cost_estimate=pl.CostEstimate(
            flops=flops, bytes_accessed=4 * 1024 * 1024, transcendentals=SLOTS * SIDE * SIDE
        ),
    )(
        object_field,
        components,
        relax_weights,
        amplitudes,
        positions,
        counts,
        *[jnp.asarray(table) for table in tables()],
    )
    return object_grad, probe_grad.reshape(1, COMP, 2, SIDE, SIDE)


def solution(mesh):
    return jax.shard_map(
        local,
        mesh=mesh,
        in_specs=(
            P(None, "tile", None),
            P("mode", None, None, None, None),
            P("tile", None),
            P("tile", None, None),
            P("tile", None),
            P("tile"),
        ),
        out_specs=(P(None, "tile", "mode"), P("mode", None, None, None, None)),
        check_vma=False,
    )
```

time: 1770 us -> 123 us (0.07)
  waiting for transfers between devices: 1570 us -> 0 us
  Pallas kernels: 0 us -> 112 us
  local copies, waits for them, and re-layouts: 105 us -> 9.27 us
  loops' own time: 27.6 us -> 0 us
  matrix products: 25.9 us -> 0 us
    psum x2 -> x0, waiting for transfers between devices: 1520 us -> none  [the longest x1 1450 us: local(): probe_grad = lax.psum(local_probe, 'tile')]
    pallas_call x0 -> x1, Pallas kernels: none -> 112 us  [local(): pl.pallas_call(functools.partial(kernel, tiles), out_shape=(jax.ShapeDtyp...]
    gather x32 -> x0, local copies, waits for them, and re-layouts: 61.6 us -> none
    reduce_scatter x1 -> x0, waiting for transfers between devices: 39.2 us -> none  [local(): lax.psum_scatter(whole_grad, 'mode', scatter_dimension=2, tiled=True)]
    another operation x2 -> x0, loops' own time: 27.6 us -> none  [the longest x1 27.6 us: local(): lax.fori_loop(0, slot_count, place_patch, jnp.zeros_like(extended))]
    dot_general x18 -> x0, matrix products: 25.9 us -> none  [the longest x8 11.8 us: on_right(): return jnp.einsum('...ab,bc->...ac', values, matrix, precision=highest)]
    dynamic_slice x24 -> x0, local copies, waits for them, and re-layouts: 19.9 us -> none  [the longest x8 10.6 us: place_patch(): patch_grad[index_slot]]
  transfers between devices with their start and end apart: 5 -> 0, of which waited for: 5 -> 0; matrix products, arithmetic and copies ran while one was open for 1% -> 0% of each run, Pallas kernels for 0% -> 0%
where the time goes in v1:
time: 123 us
  Pallas kernels  112 us (91%)
  local copies, waits for them, and re-layouts  9.27 us (8%)
  between operations  1.3 us (1%)
    pallas_call x1, Pallas kernels, local(): pl.pallas_call(functools.partial(kernel, tiles), out_shape=(jax.ShapeDtyp...  112 us
    unnamed x20, local copies, waits for them, and re-layouts  9.27 us

profile of v1, /device:TPU:1, one launch (start us, length us, event | category | flops | bytes accessed | tf_op | source)
XLA Modules:
  0.0 122.7 jit_solution(5755807128263158682)
XLA Ops:
  1.3 0.0 copy-start.7
  1.3 0.8 copy.12.weights_ref
  2.0 0.0 copy-done.7
  2.1 0.1 copy.13.positions_ref
  2.1 0.0 copy-start
  2.1 1.2 copy-done
  3.4 0.0 copy-start.1
  3.4 1.0 copy-done.1
  4.4 0.0 copy-start.2
  4.4 1.0 copy-done.2
  5.4 0.0 copy-start.3
  5.4 0.9 copy-done.3
  6.3 0.0 copy-start.4
  6.3 0.9 copy-done.4
  7.3 0.0 copy-start.5
  7.3 0.9 copy-done.5
  8.2 0.0 copy-start.6
  8.2 0.9 copy-done.6
  9.1 112.1 %shard_map.113 = (f32[2,128,256]{2,1,0:T(8,128)S(1)}, f32[1024,128]{1,0:T(8,128)S(1)}) custom-call(f32[2,128,1024]{2,1,0:T(8,128)S(1)} %copy-done, f32[1,4,2,128,128]{4,3,2,1,0:T(8,128)S(1)} %copy-done.1, f32[8,4]{1,0:T(8,128)S(1)} %copy.12.weights_ref, f32[8,128,128]{2,1,0:T(8,128)S(1)} %copy-done.2, s32[8,2]{1,0:T(8,128)S(1)} %copy.13.positions_ref, ...), custom_call_target="tpu_custom_call" | custom-call | flops 1610612736 | bytes 4194304 | tf_op jit(solution)/shard_map/pallas_call | solution.py:552
  121.2 0.7 copy.17
  121.9 0.8 copy.18
Async XLA Ops:
  1.3 0.8 copy-start.7
  2.1 1.2 copy-start
  3.4 1.0 copy-start.1
  4.4 1.0 copy-start.2
  5.4 0.9 copy-start.3
  6.3 0.9 copy-start.4
  7.3 0.9 copy-start.5
  8.2 0.9 copy-start.6

commit v2 on v1

--- a/solution.py
+++ b/solution.py
@@ -18,10 +18,13 @@
 QUARTER = 32
 HALF = 16
 EMPTY = 2 * SLOTS
+PACK = 1
+PACKS = SLOTS // PACK
+LAG = 5
 
 
 def group_size(tiles):
-    return 16 if tiles % 16 == 0 else 2
+    return 8 if tiles % 16 == 0 else 2
 
 
 def owner_count(depth):
@@ -54,12 +57,14 @@
     amplitudes_ref,
     positions_ref,
     counts_ref,
-    row_high,
-    row_low,
-    col_high,
-    col_low,
+    table_ref,
     object_out,
     probe_out,
+    weights,
+    positions,
+    counts,
+    table,
+    waves,
     ext,
     comp,
     amps,
@@ -123,7 +128,17 @@
     def columns(ref, at):
         return ref.at[:, :, pl.ds(at * SIDE, SIDE)]
 
+    barrier = pltpu.get_barrier_semaphore()
+    peers = [{"tile": above}, {"tile": below}, {"mode": right}, {"mode": left}]
+    peers += [{"tile": near(step)} for step in range(1, group)]
+    peers += [{"tile": beyond(step)} for step in range(1, depth)]
+    for peer in peers:
+        pl.semaphore_signal(barrier, inc=1, device_id=peer, device_id_type=MESH)
     loads = [
+        pltpu.make_async_copy(weights_ref, weights, local_sems.at[10]),
+        pltpu.make_async_copy(positions_ref, positions, local_sems.at[11]),
+        pltpu.make_async_copy(counts_ref, counts, local_sems.at[12]),
+        pltpu.make_async_copy(table_ref, waves, local_sems.at[13]),
         pltpu.make_async_copy(components_ref.at[0], comp, local_sems.at[0]),
         pltpu.make_async_copy(
             amplitudes_ref.at[:, pl.ds(pl.multiple_of(mode * QUARTER, 8), QUARTER), :],
@@ -138,13 +153,6 @@
     ]
     for copy in loads:
         copy.start()
-
-    barrier = pltpu.get_barrier_semaphore()
-    peers = [{"tile": above}, {"tile": below}, {"mode": right}, {"mode": left}]
-    peers += [{"tile": near(step)} for step in range(1, group)]
-    peers += [{"tile": beyond(step)} for step in range(1, depth)]
-    for peer in peers:
-        pl.semaphore_signal(barrier, inc=1, device_id=peer, device_id_type=MESH)
     pl.semaphore_wait(barrier, len(peers))
 
     halo = [
@@ -172,12 +180,21 @@
         placed[plane, EMPTY, pl.ds(SIDE, SIDE), :] = jnp.zeros((SIDE, SIDE), jnp.float32)
     for copy in loads:
         copy.wait()
+    cos_high, cos_low = split(waves[0])
+    sin_high, sin_low = split(waves[1])
+    for at, (cos, sin) in enumerate(((cos_high, sin_high), (cos_low, sin_low))):
+        lower = jnp.concatenate([-sin, cos], axis=1)
+        upper = jnp.concatenate([cos, sin], axis=1)
+        table[at] = jnp.concatenate([upper, lower], axis=0)
+        lower = jnp.concatenate([sin, cos], axis=1)
+        upper = jnp.concatenate([cos, -sin], axis=1)
+        table[2 + at] = jnp.concatenate([upper, lower], axis=0)
 
     def mix(slot, carry):
         for plane in range(2):
-            total = weights_ref[slot, 0] * comp[0, plane]
+            total = weights[0, slot] * comp[0, plane]
             for at in range(1, COMP):
-                total = total + weights_ref[slot, at] * comp[at, plane]
+                total = total + weights[at, slot] * comp[at, plane]
             probes[slot, plane] = total
         return carry
 
@@ -194,8 +211,8 @@
     lane = lax.broadcasted_iota(jnp.int32, (SIDE, SIDE), 1)
 
     def place_of(slot):
-        row = positions_ref[slot, 0] & (SIDE - 1)
-        col = positions_ref[slot, 1]
+        row = positions[0, slot] & (SIDE - 1)
+        col = positions[1, slot]
         base = jnp.minimum(lax.shift_right_logical(col, 7), TILES_WIDE - 2)
         return row, base, col - base * SIDE
 
@@ -212,57 +229,58 @@
     right_rows = pl.multiple_of(QUARTER * right, 8)
     left_rows = pl.multiple_of(QUARTER * left, 8)
 
-    def first_pass(slot):
+    def slots_of(pack):
+        return pl.ds(pack * PACK, PACK)
+
+    def first_pass(pack):
         return [
             send(
-                power.at[slot, pl.ds(ahead, QUARTER), :],
-                pair_in.at[slot, 0],
-                slot_sems.at[:, slot, 0],
+                power.at[slots_of(pack), pl.ds(ahead, QUARTER), :],
+                pair_in.at[pack, 0],
+                slot_sems.at[:, pack, 0],
                 {"mode": right},
             ),
             send(
-                power.at[slot, pl.ds(behind, QUARTER), :],
-                pair_in.at[slot, 1],
-                slot_sems.at[:, slot, 1],
+                power.at[slots_of(pack), pl.ds(behind, QUARTER), :],
+                pair_in.at[pack, 1],
+                slot_sems.at[:, pack, 1],
                 {"mode": left},
             ),
         ]
 
-    def second_pass(slot):
+    def second_pass(pack):
         return [
             send(
-                pair_mid.at[slot, 0],
-                pair_sum.at[slot, 0],
-                slot_sems.at[:, slot, 2],
+                pair_mid.at[pack, 0],
+                pair_sum.at[pack, 0],
+                slot_sems.at[:, pack, 2],
                 {"mode": right},
             ),
             send(
-                pair_mid.at[slot, 1],
-                pair_sum.at[slot, 1],
-                slot_sems.at[:, slot, 3],
+                pair_mid.at[pack, 1],
+                pair_sum.at[pack, 1],
+                slot_sems.at[:, pack, 3],
                 {"mode": left},
             ),
         ]
 
-    def factor_rows(slot, start, count):
-        return factor.at[slot, pl.ds(start, count), :]
-
-    def third_pass(slot):
-        mid = factor_rows(slot, own_rows, QUARTER)
+    def in_place(pack, start, count, kind, peer):
+        ref = factor.at[slots_of(pack), pl.ds(start, count), :]
+        return send(ref, ref, slot_sems.at[:, pack, kind], {"mode": peer})
+
+    def third_pass(pack, start_right=own_rows, start_left=own_rows):
         return [
-            send(mid, mid, slot_sems.at[:, slot, 4], {"mode": right}),
-            send(mid, mid, slot_sems.at[:, slot, 5], {"mode": left}),
+            in_place(pack, start_right, QUARTER, 4, right),
+            in_place(pack, start_left, QUARTER, 5, left),
         ]
 
-    def fourth_pass(slot):
-        top = factor_rows(slot, left_rows, HALF)
-        bottom = factor_rows(slot, pl.multiple_of(right_rows + HALF, 8), HALF)
+    def fourth_pass(pack, top=left_rows, bottom=right_rows):
         return [
-            send(top, top, slot_sems.at[:, slot, 6], {"mode": right}),
-            send(bottom, bottom, slot_sems.at[:, slot, 7], {"mode": left}),
+            in_place(pack, top, HALF, 6, right),
+            in_place(pack, pl.multiple_of(bottom + HALF, 8), HALF, 7, left),
         ]
 
-    def forward(slot):
+    def forward(slot, carry):
         for plane in range(2):
             patches[slot, plane] = take(slot, plane)
         probe_re, probe_im = probes[slot, 0], probes[slot, 1]
@@ -274,58 +292,61 @@
             ],
             axis=1,
         )
-        wave = both_sides(wide, row_high[...], row_low[...], col_high[...], col_low[...])
+        wave = both_sides(wide, table[0], table[1], table[2], table[3])
         far[slot] = wave
         strength = wave[:SIDE] * wave[:SIDE] + wave[SIDE:] * wave[SIDE:]
         power[slot, pl.ds(0, SIDE), :] = strength
         power[slot, pl.ds(SIDE, HALF), :] = strength[:HALF]
-        for copy in first_pass(slot):
+        return carry
+
+    def send_power(pack):
+        lax.fori_loop(pack * PACK, pack * PACK + PACK, forward, 0)
+        for copy in first_pass(pack):
             copy.start()
 
-    def relay_power(slot):
-        to_right, to_left = first_pass(slot)
-        go_right, go_left = second_pass(slot)
+    def relay_power(pack):
+        slots = slots_of(pack)
+        to_right, to_left = first_pass(pack)
+        go_right, go_left = second_pass(pack)
         to_right.wait_recv()
-        pair_mid[slot, 0] = pair_in[slot, 0, pl.ds(HALF, HALF), :] + power[slot, pl.ds(right_rows, HALF), :]
+        pair_mid[pack, 0] = (
+            pair_in[pack, 0, :, pl.ds(HALF, HALF), :] + power[slots, pl.ds(right_rows, HALF), :]
+        )
         go_right.start()
         to_left.wait_recv()
-        pair_mid[slot, 1] = (
-            pair_in[slot, 1, pl.ds(0, HALF), :]
-            + power[slot, pl.ds(pl.multiple_of(left_rows + HALF, 8), HALF), :]
+        pair_mid[pack, 1] = (
+            pair_in[pack, 1, :, pl.ds(0, HALF), :]
+            + power[slots, pl.ds(pl.multiple_of(left_rows + HALF, 8), HALF), :]
         )
         go_left.start()
 
-    def make_factor(slot):
-        for copy in second_pass(slot):
+    def make_factor(pack):
+        for copy in second_pass(pack):
             copy.wait_recv()
-        own = power[slot, pl.ds(own_rows, QUARTER), :]
-        top = own[:HALF] + pair_sum[slot, 0] + pair_in[slot, 1, pl.ds(HALF, HALF), :]
-        bottom = own[HALF:] + pair_sum[slot, 1] + pair_in[slot, 0, pl.ds(0, HALF), :]
-        intensity = jnp.concatenate([top, bottom], axis=0)
-        ratio = 1.0 - amps[slot] * lax.rsqrt(jnp.maximum(intensity, 1.0))
-        factor[slot, pl.ds(own_rows, QUARTER), :] = jnp.where(slot < counts_ref[0], ratio, 0.0)
-        for copy in third_pass(slot):
+        for inner in range(PACK):
+            slot = pack * PACK + inner
+            own = power[slot, pl.ds(own_rows, QUARTER), :]
+            top = own[:HALF] + pair_sum[pack, 0, inner] + pair_in[pack, 1, inner, pl.ds(HALF, HALF), :]
+            bottom = own[HALF:] + pair_sum[pack, 1, inner] + pair_in[pack, 0, inner, pl.ds(0, HALF), :]
+            intensity = jnp.concatenate([top, bottom], axis=0)
+            ratio = 1.0 - amps[slot] * lax.rsqrt(jnp.maximum(intensity, 1.0))
+            factor[slot, pl.ds(own_rows, QUARTER), :] = jnp.where(slot < counts[0], ratio, 0.0)
+        for copy in third_pass(pack):
             copy.start()
 
-    def relay_factor(slot):
-        go_right, go_left = fourth_pass(slot)
-        from_left = factor_rows(slot, left_rows, QUARTER)
-        send(from_left, from_left, slot_sems.at[:, slot, 4], {"mode": right}).wait_recv()
+    def relay_factor(pack):
+        from_left, from_right = third_pass(pack, left_rows, right_rows)
+        go_right, go_left = fourth_pass(pack)
+        from_left.wait_recv()
         go_right.start()
-        from_right = factor_rows(slot, right_rows, QUARTER)
-        send(from_right, from_right, slot_sems.at[:, slot, 5], {"mode": left}).wait_recv()
+        from_right.wait_recv()
         go_left.start()
 
-    def backward(slot):
-        across = pl.multiple_of(QUARTER * lax.rem(mode + 2, MODES), 8)
-        top = factor_rows(slot, across, HALF)
-        send(top, top, slot_sems.at[:, slot, 6], {"mode": right}).wait_recv()
-        bottom = factor_rows(slot, pl.multiple_of(across + HALF, 8), HALF)
-        send(bottom, bottom, slot_sems.at[:, slot, 7], {"mode": left}).wait_recv()
+    def backward(slot, carry):
         scale = factor[slot]
         wave = far[slot]
         wide = jnp.concatenate([wave[:SIDE] * scale, wave[SIDE:] * scale], axis=1)
-        back = both_sides(wide, col_high[...], col_low[...], row_high[...], row_low[...])
+        back = both_sides(wide, table[2], table[3], table[0], table[1])
         back_re, back_im = back[:SIDE], back[SIDE:]
         probe_re, probe_im = probes[slot, 0], probes[slot, 1]
         shift = place_of(slot)[2]
@@ -345,20 +366,28 @@
         for at in range(COMP):
             for plane in range(2):
                 where_at = pl.ds((2 * at + plane) * SIDE, SIDE)
-                terms[where_at, :] = terms[where_at, :] + weights_ref[slot, at] * pieces[plane]
-
-    stages = (forward, relay_power, make_factor, relay_factor, backward)
+                terms[where_at, :] = terms[where_at, :] + weights[at, slot] * pieces[plane]
+        return carry
+
+    def use_factor(pack):
+        across = pl.multiple_of(QUARTER * lax.rem(mode + 2, MODES), 8)
+        for copy in fourth_pass(pack, across, across):
+            copy.wait_recv()
+        lax.fori_loop(pack * PACK, pack * PACK + PACK, backward, 0)
+
+    stages = (send_power, relay_power, make_factor, relay_factor, use_factor)
 
     def step(at, carry):
-        for lag, stage in enumerate(stages):
-
-            @pl.when((at >= lag) & (at < SLOTS + lag))
+        for place, stage in enumerate(stages):
+            lag = place * LAG
+
+            @pl.when((at >= lag) & (at < PACKS + lag))
             def _():
                 stage(at - lag)
 
         return carry
 
-    lax.fori_loop(0, SLOTS + len(stages) - 1, step, 0)
+    lax.fori_loop(0, PACKS + (len(stages) - 1) * LAG, step, 0)
 
     def gathered(plane, tile_at, start):
         total = None
@@ -515,13 +544,13 @@
         for step in range(1, depth):
             from_owner(level, step).wait_send()
 
-    def settle(slot, carry):
+    def settle(pack, carry):
         for make in (first_pass, second_pass, third_pass, fourth_pass):
-            for copy in make(slot):
+            for copy in make(pack):
                 copy.wait_send()
         return carry
 
-    lax.fori_loop(0, SLOTS, settle, 0)
+    lax.fori_loop(0, PACKS, settle, 0)
 
 
 def tables():
@@ -529,13 +558,7 @@
     angle = (line[:, None] * line[None, :] % SIDE) * (2.0 * math.pi / SIDE)
     cos = np.cos(angle) / math.sqrt(SIDE)
     sin = -np.sin(angle) / math.sqrt(SIDE)
-    row = np.block([[cos, sin], [-sin, cos]])
-    kinds = []
-    for full in (row, row.T):
-        high = full.astype(np.float32).astype(jnp.bfloat16)
-        low = (full - high.astype(np.float64)).astype(np.float32).astype(jnp.bfloat16)
-        kinds += [high, low]
-    return kinds
+    return np.stack([cos, sin]).astype(np.float32)
 
 
 def local(object_field, components, relax_weights, amplitudes, positions, counts):
@@ -545,8 +568,7 @@
     rows = COMP * 2 * SIDE // group
     piece = rows // owner_count(depth)
     f32 = jnp.float32
-    anywhere = pl.BlockSpec(memory_space=pl.ANY)
-    scalars = pl.BlockSpec(memory_space=pltpu.SMEM)
+    anywhere = pl.BlockSpec(memory_space=pltpu.HBM)
     vector = pl.BlockSpec(memory_space=pltpu.VMEM)
     flops = 2 * 2 * SLOTS * 3 * 2 * 256 * 256 * 128
     object_grad, probe_grad = pl.pallas_call(
@@ -555,9 +577,14 @@
             jax.ShapeDtypeStruct((2, SIDE, 2 * SIDE), f32),
             jax.ShapeDtypeStruct((COMP * 2 * SIDE, SIDE), f32),
         ),
-        in_specs=[anywhere, anywhere, scalars, anywhere, scalars, scalars] + [vector] * 4,
+        in_specs=[anywhere] * 7,
         out_specs=(vector, vector),
         scratch_shapes=[
+            pltpu.SMEM((COMP, SLOTS), f32),
+            pltpu.SMEM((2, SLOTS), jnp.int32),
+            pltpu.SMEM((1,), jnp.int32),
+            pltpu.VMEM((4, 2 * SIDE, 2 * SIDE), jnp.bfloat16),
+            pltpu.VMEM((2, SIDE, SIDE), f32),
             pltpu.VMEM((2, TILES_WIDE, 2 * SIDE, SIDE), f32),
             pltpu.VMEM((COMP, 2, SIDE, SIDE), f32),
             pltpu.VMEM((SLOTS, QUARTER, SIDE), f32),
@@ -565,9 +592,9 @@
             pltpu.VMEM((SLOTS, 2, SIDE, SIDE), f32),
             pltpu.VMEM((SLOTS, 2 * SIDE, SIDE), f32),
             pltpu.VMEM((SLOTS, SIDE + HALF, SIDE), f32),
-            pltpu.VMEM((SLOTS, 2, QUARTER, SIDE), f32),
-            pltpu.VMEM((SLOTS, 2, HALF, SIDE), f32),
-            pltpu.VMEM((SLOTS, 2, HALF, SIDE), f32),
+            pltpu.VMEM((PACKS, 2, PACK, QUARTER, SIDE), f32),
+            pltpu.VMEM((PACKS, 2, PACK, HALF, SIDE), f32),
+            pltpu.VMEM((PACKS, 2, PACK, HALF, SIDE), f32),
             pltpu.VMEM((SLOTS, SIDE, SIDE), f32),
             pltpu.VMEM((2, EMPTY + 1, 3 * SIDE, SIDE), f32),
             pltpu.VMEM((8, 2, SIDE, SIDE), f32),
@@ -578,9 +605,9 @@
             pltpu.VMEM((rows, SIDE), f32),
             pltpu.VMEM((group, rows, SIDE), f32),
             pltpu.VMEM((depth, piece, SIDE), f32),
-            pltpu.SemaphoreType.DMA((2 + TILES_WIDE,)),
+            pltpu.SemaphoreType.DMA((6 + TILES_WIDE,)),
             pltpu.SemaphoreType.DMA((2, TILES_WIDE)),
-            pltpu.SemaphoreType.DMA((2, SLOTS, 8)),
+            pltpu.SemaphoreType.DMA((2, PACKS, 8)),
             pltpu.SemaphoreType.DMA((2, 8)),
             pltpu.SemaphoreType.DMA((2, 6)),
             pltpu.SemaphoreType.DMA((2, group)),
@@ -589,7 +616,7 @@
             pltpu.SemaphoreType.DMA((2, group)),
         ],
         compiler_params=pltpu.CompilerParams(
-            collective_id=0, has_side_effects=True, vmem_limit_bytes=48 * 1024 * 1024
+            collective_id=0, has_side_effects=True, vmem_limit_bytes=62 * 1024 * 1024
         ),
         cost_estimate=pl.CostEstimate(
             flops=flops, bytes_accessed=4 * 1024 * 1024, transcendentals=SLOTS * SIDE * SIDE
@@ -597,11 +624,11 @@
     )(
         object_field,
         components,
-        relax_weights,
+        relax_weights.T,
         amplitudes,
-        positions,
+        positions.T,
         counts,
-        *[jnp.asarray(table) for table in tables()],
+        jnp.asarray(tables()),
     )
     return object_grad, probe_grad.reshape(1, COMP, 2, SIDE, SIDE)
 

time: 123 us -> 106 us (0.86)
  Pallas kernels: 112 us -> 102 us
  local copies, waits for them, and re-layouts: 9.27 us -> 2.52 us
    pallas_call x1, Pallas kernels: 112 us -> 102 us  [local(): pl.pallas_call(functools.partial(kernel, tiles), out_shape=(jax.ShapeDtyp...]
    unnamed x20 -> x4, local copies, waits for them, and re-layouts: 9.27 us -> 2.52 us
where the time goes in v2:
time: 106 us
  Pallas kernels  102 us (96%)
  local copies, waits for them, and re-layouts  2.52 us (2%)
  between operations  1.29 us (1%)
    pallas_call x1, Pallas kernels, local(): pl.pallas_call(functools.partial(kernel, tiles), out_shape=(jax.ShapeDtyp...  102 us
    unnamed x4, local copies, waits for them, and re-layouts  2.52 us

profile of v2, /device:TPU:1, one launch (start us, length us, event | category | flops | bytes accessed | tf_op | source)
XLA Modules:
  0.0 105.6 jit_solution(14086491327169790968)
XLA Ops:
  1.3 101.7 %shard_map.86 = (f32[2,128,256]{2,1,0:T(8,128)}, f32[1024,128]{1,0:T(8,128)}) custom-call(f32[2,128,1024]{2,1,0:T(8,128)} %object_ref.1, f32[1,4,2,128,128]{4,3,2,1,0:T(8,128)} %components_ref.1, f32[4,8]{1,0:T(4,128)} %bitcast.4, f32[8,128,128]{2,1,0:T(8,128)} %amplitudes_ref.1, s32[2,8]{1,0:T(2,128)} %bitcast.5, s32[1]{0:T(128)S(6)} %copy.11.counts_ref, ...), custom_call_target="tpu_custom_call" | custom-call | flops 1610612736 | bytes 4194304 | tf_op jit(solution)/shard_map/pallas_call | solution.py:574
  103.0 0.0 copy-start
  103.0 1.7 %copy.12 = f32[2,128,256]{2,1,0:T(8,128)} copy(f32[2,128,256]{2,1,0:T(8,128)} %get-tuple-element.8) | data formatting | bytes 524288
  104.8 0.0 copy-done
  104.8 0.8 copy.13
Async XLA Ops:
  103.0 1.7 %copy-start = (f32[1024,128]{1,0:T(8,128)S(1)}, f32[1024,128]{1,0:T(8,128)}, u32[]{:S(2)}) copy-start(f32[1024,128]{1,0:T(8,128)} %get-tuple-element.5) | copy-start | bytes 1572868

commit v3 on v2

--- a/solution.py
+++ b/solution.py
@@ -18,13 +18,13 @@
 QUARTER = 32
 HALF = 16
 EMPTY = 2 * SLOTS
-PACK = 1
+PACK = 2
 PACKS = SLOTS // PACK
-LAG = 5
+LAG = 3
 
 
 def group_size(tiles):
-    return 8 if tiles % 16 == 0 else 2
+    return 8 if tiles % 16 == 0 else 4
 
 
 def owner_count(depth):
@@ -82,6 +82,8 @@
     part,
     part_in,
     terms,
+    half_in,
+    half_sum,
     chunk,
     near_buf,
     far_buf,
@@ -90,6 +92,7 @@
     slot_sems,
     rim_sems,
     part_sems,
+    pair_sems,
     near_sems,
     far_sems,
     back_sems,
@@ -109,8 +112,15 @@
     mine = lax.rem(tile, group)
     level = lax.div(tile, group)
 
+    across = group // 2
+    core = lax.rem(mine, 2)
+    chip = lax.div(mine, 2)
+    place = core * across + chip
+    sibling = level * group + chip * 2 + 1 - core
+    half_rows = COMP * SIDE
+
     def near(step):
-        return level * group + lax.rem(mine + step, group)
+        return level * group + lax.rem(chip + step, across) * 2 + core
 
     def beyond(step):
         return lax.rem(level + step, depth) * group + mine
@@ -130,7 +140,8 @@
 
     barrier = pltpu.get_barrier_semaphore()
     peers = [{"tile": above}, {"tile": below}, {"mode": right}, {"mode": left}]
-    peers += [{"tile": near(step)} for step in range(1, group)]
+    peers += [{"tile": sibling}]
+    peers += [{"tile": near(step)} for step in range(1, across)]
     peers += [{"tile": beyond(step)} for step in range(1, depth)]
     for peer in peers:
         pl.semaphore_signal(barrier, inc=1, device_id=peer, device_id_type=MESH)
@@ -280,7 +291,7 @@
             in_place(pack, pl.multiple_of(bottom + HALF, 8), HALF, 7, left),
         ]
 
-    def forward(slot, carry):
+    def forward(slot):
         for plane in range(2):
             patches[slot, plane] = take(slot, plane)
         probe_re, probe_im = probes[slot, 0], probes[slot, 1]
@@ -297,10 +308,10 @@
         strength = wave[:SIDE] * wave[:SIDE] + wave[SIDE:] * wave[SIDE:]
         power[slot, pl.ds(0, SIDE), :] = strength
         power[slot, pl.ds(SIDE, HALF), :] = strength[:HALF]
-        return carry
 
     def send_power(pack):
-        lax.fori_loop(pack * PACK, pack * PACK + PACK, forward, 0)
+        for inner in range(PACK):
+            forward(pack * PACK + inner)
         for copy in first_pass(pack):
             copy.start()
 
@@ -342,7 +353,7 @@
         from_right.wait_recv()
         go_left.start()
 
-    def backward(slot, carry):
+    def backward(slot):
         scale = factor[slot]
         wave = far[slot]
         wide = jnp.concatenate([wave[:SIDE] * scale, wave[SIDE:] * scale], axis=1)
@@ -367,13 +378,13 @@
             for plane in range(2):
                 where_at = pl.ds((2 * at + plane) * SIDE, SIDE)
                 terms[where_at, :] = terms[where_at, :] + weights[at, slot] * pieces[plane]
-        return carry
 
     def use_factor(pack):
-        across = pl.multiple_of(QUARTER * lax.rem(mode + 2, MODES), 8)
-        for copy in fourth_pass(pack, across, across):
+        facing = pl.multiple_of(QUARTER * lax.rem(mode + 2, MODES), 8)
+        for copy in fourth_pass(pack, facing, facing):
             copy.wait_recv()
-        lax.fori_loop(pack * PACK, pack * PACK + PACK, backward, 0)
+        for inner in range(PACK):
+            backward(pack * PACK + inner)
 
     stages = (send_power, relay_power, make_factor, relay_factor, use_factor)
 
@@ -406,29 +417,40 @@
         turn, plane = order[at]
         return lax.rem(mode + turn, MODES), plane
 
-    rims = []
-    for at in range(8):
-        block, plane = block_of(at)
-        for half in range(2):
-            rim_out[at, half] = gathered(plane, 2 * block + half, 2 * SIDE)
-        copy = send(rim_out.at[at], rim_in.at[at], rim_sems.at[:, at], {"tile": below})
-        copy.start()
-        rims.append(copy)
-
     def chunk_rows(at):
         return pl.ds(pl.multiple_of(at * rows, 8), rows)
 
-    spread = [
-        send(
-            terms.at[chunk_rows(lax.rem(mine + step, group))],
+    def half_of(ref, at):
+        return ref.at[pl.ds(pl.multiple_of(at * half_rows, 8), half_rows)]
+
+    halves = send(half_of(terms, 1 - core), half_in, pair_sems.at[:, 0], {"tile": sibling})
+    halves.start()
+
+    rims = []
+
+    def send_rims(start, stop):
+        for at in range(start, stop):
+            block, plane = block_of(at)
+            for half in range(2):
+                rim_out[at, half] = gathered(plane, 2 * block + half, 2 * SIDE)
+            copy = send(rim_out.at[at], rim_in.at[at], rim_sems.at[:, at], {"tile": below})
+            copy.start()
+            rims.append(copy)
+
+    send_rims(0, 2)
+    halves.wait_recv()
+    half_sum[...] = terms[pl.ds(pl.multiple_of(core * half_rows, 8), half_rows), :] + half_in[...]
+    spread = []
+    for step in range(1, across):
+        copy = send(
+            half_sum.at[chunk_rows(lax.rem(chip + step, across))],
             near_buf.at[step],
             near_sems.at[:, step],
             {"tile": near(step)},
         )
-        for step in range(1, group)
-    ]
-    for copy in spread:
         copy.start()
+        spread.append(copy)
+    send_rims(2, 8)
 
     part_peers = ({"mode": right}, {"mode": left})
     part_kind = (0, 2, 1, 3, 4, 5)
@@ -456,18 +478,6 @@
                 value = value + part_in[kind, half]
             yield half, value
 
-    for at in range(4):
-        for half, value in whole(at, ()):
-            part[at, half] = value
-        parts[at].start()
-
-    for copy in spread:
-        copy.wait_recv()
-    total = terms[chunk_rows(mine), :]
-    for step in range(1, group):
-        total = total + near_buf[step]
-    chunk[...] = total
-
     def to_owner(step):
         target = lax.rem(level + step, depth)
         at = pl.ds(pl.multiple_of(lax.rem(target, owners) * piece, 8), piece)
@@ -476,10 +486,22 @@
         )
 
     def from_owner(source, step):
-        at = pl.ds(pl.multiple_of(mine * rows + lax.rem(source, owners) * piece, 8), piece)
+        at = pl.ds(pl.multiple_of(place * rows + lax.rem(source, owners) * piece, 8), piece)
         return send(
             probe_out.at[at], probe_out.at[at], back_sems.at[:, step], {"tile": beyond(step)}
         )
+
+    for at in range(0, 2):
+        for half, value in whole(at, ()):
+            part[at, half] = value
+        parts[at].start()
+
+    for copy in spread:
+        copy.wait_recv()
+    total = half_sum[chunk_rows(chip), :]
+    for step in range(1, across):
+        total = total + near_buf[step]
+    chunk[...] = total
 
     for step in range(1, depth):
         target, copy = to_owner(step)
@@ -488,8 +510,8 @@
         def _():
             copy.start()
 
-    for at in range(4, 6):
-        for half, value in whole(at, (2 * (at - 4),)):
+    for at in range(2, 4):
+        for half, value in whole(at, ()):
             part[at, half] = value
         parts[at].start()
 
@@ -500,10 +522,15 @@
         total = chunk[pl.ds(pl.multiple_of(lax.rem(level, owners) * piece, 8), piece), :]
         for step in range(1, depth):
             total = total + far_buf[step]
-        at = pl.ds(pl.multiple_of(mine * rows + lax.rem(level, owners) * piece, 8), piece)
+        at = pl.ds(pl.multiple_of(place * rows + lax.rem(level, owners) * piece, 8), piece)
         probe_out[at, :] = total
         for step in range(1, depth):
             from_owner(level, step).start()
+
+    for at in range(4, 6):
+        for half, value in whole(at, (2 * (at - 4),)):
+            part[at, half] = value
+        parts[at].start()
 
     for step in range(1, depth):
         source = lax.rem(level - step + depth, depth)
@@ -518,20 +545,31 @@
             probe_out.at[at], probe_out.at[at], spread_sems.at[:, step], {"tile": near(step)}
         )
 
-    for step in range(1, group):
-        shared(mine, step).start()
-
-    for at in range(6, 8):
+    for step in range(1, across):
+        shared(place, step).start()
+
+    for at in range(6, 7):
         for half, value in whole(at, (4, 3) if at == 6 else (5, 1)):
             object_out[at - 6, :, pl.ds(half * SIDE, SIDE)] = value
 
-    for step in range(1, group):
-        shared(lax.rem(mine - step + group, group), step).wait_recv()
-
+    for step in range(1, across):
+        shared(core * across + lax.rem(chip - step + across, across), step).wait_recv()
+
+    def final(at):
+        ref = half_of(probe_out, at)
+        return send(ref, ref, pair_sems.at[:, 1], {"tile": sibling})
+
+    final(core).start()
+    for at in range(7, 8):
+        for half, value in whole(at, (4, 3) if at == 6 else (5, 1)):
+            object_out[at - 6, :, pl.ds(half * SIDE, SIDE)] = value
+    final(1 - core).wait_recv()
+    final(core).wait_send()
+    halves.wait_send()
     for copy in halo + rims + parts + spread:
         copy.wait_send()
-    for step in range(1, group):
-        shared(mine, step).wait_send()
+    for step in range(1, across):
+        shared(place, step).wait_send()
     for step in range(1, depth):
         target, copy = to_owner(step)
 
@@ -602,18 +640,21 @@
             pltpu.VMEM((6, 2, SIDE, SIDE), f32),
             pltpu.VMEM((6, 2, SIDE, SIDE), f32),
             pltpu.VMEM((COMP * 2 * SIDE, SIDE), f32),
+            pltpu.VMEM((COMP * SIDE, SIDE), f32),
+            pltpu.VMEM((COMP * SIDE, SIDE), f32),
             pltpu.VMEM((rows, SIDE), f32),
-            pltpu.VMEM((group, rows, SIDE), f32),
+            pltpu.VMEM((group // 2, rows, SIDE), f32),
             pltpu.VMEM((depth, piece, SIDE), f32),
             pltpu.SemaphoreType.DMA((6 + TILES_WIDE,)),
             pltpu.SemaphoreType.DMA((2, TILES_WIDE)),
             pltpu.SemaphoreType.DMA((2, PACKS, 8)),
             pltpu.SemaphoreType.DMA((2, 8)),
             pltpu.SemaphoreType.DMA((2, 6)),
-            pltpu.SemaphoreType.DMA((2, group)),
+            pltpu.SemaphoreType.DMA((2, 2)),
+            pltpu.SemaphoreType.DMA((2, group // 2)),
             pltpu.SemaphoreType.DMA((2, depth)),
             pltpu.SemaphoreType.DMA((2, depth)),
-            pltpu.SemaphoreType.DMA((2, group)),
+            pltpu.SemaphoreType.DMA((2, group // 2)),
         ],
         compiler_params=pltpu.CompilerParams(
             collective_id=0, has_side_effects=True, vmem_limit_bytes=62 * 1024 * 1024

time: 106 us -> 99.1 us (0.935)
  Pallas kernels: 102 us -> 95.1 us
    pallas_call x1, Pallas kernels: 102 us -> 95.1 us  [local(): pl.pallas_call(functools.partial(kernel, tiles), out_shape=(jax.ShapeDtyp...]
where the time goes in v3:
time: 99.1 us; the launch traced here: 98.9 us
  Pallas kernels  95.1 us (96%)
  local copies, waits for them, and re-layouts  2.52 us (3%)
  between operations  1.29 us (1%)
    pallas_call x1, Pallas kernels, local(): pl.pallas_call(functools.partial(kernel, tiles), out_shape=(jax.ShapeDtyp...  95.1 us
    unnamed x4, local copies, waits for them, and re-layouts  2.52 us

profile of v3, /device:TPU:1, one launch (start us, length us, event | category | flops | bytes accessed | tf_op | source)
XLA Modules:
  0.0 98.9 jit_solution(1564968294293571462)
XLA Ops:
  1.3 95.1 %shard_map.86 = (f32[2,128,256]{2,1,0:T(8,128)}, f32[1024,128]{1,0:T(8,128)}) custom-call(f32[2,128,1024]{2,1,0:T(8,128)} %object_ref.1, f32[1,4,2,128,128]{4,3,2,1,0:T(8,128)} %components_ref.1, f32[4,8]{1,0:T(4,128)} %bitcast.4, f32[8,128,128]{2,1,0:T(8,128)} %amplitudes_ref.1, s32[2,8]{1,0:T(2,128)} %bitcast.5, s32[1]{0:T(128)S(6)} %copy.11.counts_ref, ...), custom_call_target="tpu_custom_call" | custom-call | flops 1610612736 | bytes 4194304 | tf_op jit(solution)/shard_map/pallas_call | solution.py:612
  96.4 0.0 copy-start
  96.4 1.7 %copy.12 = f32[2,128,256]{2,1,0:T(8,128)} copy(f32[2,128,256]{2,1,0:T(8,128)} %get-tuple-element.8) | data formatting | bytes 524288
  98.1 0.0 copy-done
  98.1 0.8 copy.13
Async XLA Ops:
  96.4 1.7 %copy-start = (f32[1024,128]{1,0:T(8,128)S(1)}, f32[1024,128]{1,0:T(8,128)}, u32[]{:S(2)}) copy-start(f32[1024,128]{1,0:T(8,128)} %get-tuple-element.5) | copy-start | bytes 1572868

commit v4 on v3

--- a/solution.py
+++ b/solution.py
@@ -20,7 +20,7 @@
 EMPTY = 2 * SLOTS
 PACK = 2
 PACKS = SLOTS // PACK
-LAG = 3
+LAGS = (0, 3, 6, 9, 12)
 
 
 def group_size(tiles):
@@ -44,7 +44,10 @@
 def both_sides(wide, right_high, right_low, left_high, left_low):
     high, low = split(wide)
     middle = dot(high, right_high) + dot(low, right_high) + dot(high, right_low)
-    tall = jnp.concatenate([middle[:, :SIDE], middle[:, SIDE:]], axis=0)
+    count = wide.shape[0] // SIDE
+    blocks = [middle[at * SIDE : (at + 1) * SIDE] for at in range(count)]
+    columns = [jnp.concatenate([block[:, :SIDE], block[:, SIDE:]], axis=0) for block in blocks]
+    tall = jnp.concatenate(columns, axis=1)
     high, low = split(tall)
     return dot(left_high, high) + dot(left_high, low) + dot(left_low, high)
 
@@ -291,27 +294,32 @@
             in_place(pack, pl.multiple_of(bottom + HALF, 8), HALF, 7, left),
         ]
 
-    def forward(slot):
+    def exit_wave(slot):
         for plane in range(2):
             patches[slot, plane] = take(slot, plane)
         probe_re, probe_im = probes[slot, 0], probes[slot, 1]
         patch_re, patch_im = patches[slot, 0], patches[slot, 1]
-        wide = jnp.concatenate(
+        return jnp.concatenate(
             [
                 probe_re * patch_re - probe_im * patch_im,
                 probe_re * patch_im + probe_im * patch_re,
             ],
             axis=1,
         )
-        wave = both_sides(wide, table[0], table[1], table[2], table[3])
-        far[slot] = wave
-        strength = wave[:SIDE] * wave[:SIDE] + wave[SIDE:] * wave[SIDE:]
-        power[slot, pl.ds(0, SIDE), :] = strength
-        power[slot, pl.ds(SIDE, HALF), :] = strength[:HALF]
+
+    def forward(pack):
+        slots = [pack * PACK + inner for inner in range(PACK)]
+        wide = jnp.concatenate([exit_wave(slot) for slot in slots], axis=0)
+        waves_out = both_sides(wide, table[0], table[1], table[2], table[3])
+        for inner, slot in enumerate(slots):
+            wave = waves_out[:, inner * SIDE : (inner + 1) * SIDE]
+            far[slot] = wave
+            strength = wave[:SIDE] * wave[:SIDE] + wave[SIDE:] * wave[SIDE:]
+            power[slot, pl.ds(0, SIDE), :] = strength
+            power[slot, pl.ds(SIDE, HALF), :] = strength[:HALF]
 
     def send_power(pack):
-        for inner in range(PACK):
-            forward(pack * PACK + inner)
+        forward(pack)
         for copy in first_pass(pack):
             copy.start()
 
@@ -353,11 +361,19 @@
         from_right.wait_recv()
         go_left.start()
 
-    def backward(slot):
+    def residue(slot):
         scale = factor[slot]
         wave = far[slot]
-        wide = jnp.concatenate([wave[:SIDE] * scale, wave[SIDE:] * scale], axis=1)
-        back = both_sides(wide, table[2], table[3], table[0], table[1])
+        return jnp.concatenate([wave[:SIDE] * scale, wave[SIDE:] * scale], axis=1)
+
+    def backward(pack):
+        slots = [pack * PACK + inner for inner in range(PACK)]
+        wide = jnp.concatenate([residue(slot) for slot in slots], axis=0)
+        backs = both_sides(wide, table[2], table[3], table[0], table[1])
+        for inner, slot in enumerate(slots):
+            add_gradients(slot, backs[:, inner * SIDE : (inner + 1) * SIDE])
+
+    def add_gradients(slot, back):
         back_re, back_im = back[:SIDE], back[SIDE:]
         probe_re, probe_im = probes[slot, 0], probes[slot, 1]
         shift = place_of(slot)[2]
@@ -383,14 +399,13 @@
         facing = pl.multiple_of(QUARTER * lax.rem(mode + 2, MODES), 8)
         for copy in fourth_pass(pack, facing, facing):
             copy.wait_recv()
-        for inner in range(PACK):
-            backward(pack * PACK + inner)
+        backward(pack)
 
     stages = (send_power, relay_power, make_factor, relay_factor, use_factor)
 
     def step(at, carry):
         for place, stage in enumerate(stages):
-            lag = place * LAG
+            lag = LAGS[place]
 
             @pl.when((at >= lag) & (at < PACKS + lag))
             def _():
@@ -398,7 +413,7 @@
 
         return carry
 
-    lax.fori_loop(0, PACKS + (len(stages) - 1) * LAG, step, 0)
+    lax.fori_loop(0, PACKS + LAGS[-1], step, 0)
 
     def gathered(plane, tile_at, start):
         total = None
@@ -433,9 +448,14 @@
             block, plane = block_of(at)
             for half in range(2):
                 rim_out[at, half] = gathered(plane, 2 * block + half, 2 * SIDE)
-            copy = send(rim_out.at[at], rim_in.at[at], rim_sems.at[:, at], {"tile": below})
-            copy.start()
-            rims.append(copy)
+                copy = send(
+                    rim_out.at[at, half],
+                    rim_in.at[at, half],
+                    rim_sems.at[:, at, half],
+                    {"tile": below},
+                )
+                copy.start()
+                rims.append(copy)
 
     send_rims(0, 2)
     halves.wait_recv()
@@ -457,21 +477,22 @@
     part_side = (0, 1, 0, 1, 0, 1)
     parts = [
         send(
-            part.at[at],
-            part_in.at[part_kind[at]],
-            part_sems.at[:, part_kind[at]],
+            part.at[at, half],
+            part_in.at[part_kind[at], half],
+            part_sems.at[:, part_kind[at], half],
             part_peers[part_side[at]],
         )
         for at in range(6)
+        for half in range(2)
     ]
-    arrivals = {part_kind[at]: parts[at] for at in range(6)}
+    arrivals = {part_kind[at]: parts[2 * at : 2 * at + 2] for at in range(6)}
 
     def whole(at, extra):
         block, plane = block_of(at)
-        rims[at].wait_recv()
-        for kind in extra:
-            arrivals[kind].wait_recv()
         for half in range(2):
+            rims[2 * at + half].wait_recv()
+            for kind in extra:
+                arrivals[kind][half].wait_recv()
             value = gathered(plane, 2 * block + half, SIDE)
             value = value + jnp.where(tile > 0, rim_in[at, half], 0.0)
             for kind in extra:
@@ -494,7 +515,7 @@
     for at in range(0, 2):
         for half, value in whole(at, ()):
             part[at, half] = value
-        parts[at].start()
+            parts[2 * at + half].start()
 
     for copy in spread:
         copy.wait_recv()
@@ -513,7 +534,7 @@
     for at in range(2, 4):
         for half, value in whole(at, ()):
             part[at, half] = value
-        parts[at].start()
+            parts[2 * at + half].start()
 
     @pl.when(level < owners)
     def _():
@@ -530,7 +551,7 @@
     for at in range(4, 6):
         for half, value in whole(at, (2 * (at - 4),)):
             part[at, half] = value
-        parts[at].start()
+            parts[2 * at + half].start()
 
     for step in range(1, depth):
         source = lax.rem(level - step + depth, depth)
@@ -548,10 +569,6 @@
     for step in range(1, across):
         shared(place, step).start()
 
-    for at in range(6, 7):
-        for half, value in whole(at, (4, 3) if at == 6 else (5, 1)):
-            object_out[at - 6, :, pl.ds(half * SIDE, SIDE)] = value
-
     for step in range(1, across):
         shared(core * across + lax.rem(chip - step + across, across), step).wait_recv()
 
@@ -560,7 +577,7 @@
         return send(ref, ref, pair_sems.at[:, 1], {"tile": sibling})
 
     final(core).start()
-    for at in range(7, 8):
+    for at in range(6, 8):
         for half, value in whole(at, (4, 3) if at == 6 else (5, 1)):
             object_out[at - 6, :, pl.ds(half * SIDE, SIDE)] = value
     final(1 - core).wait_recv()
@@ -648,8 +665,8 @@
             pltpu.SemaphoreType.DMA((6 + TILES_WIDE,)),
             pltpu.SemaphoreType.DMA((2, TILES_WIDE)),
             pltpu.SemaphoreType.DMA((2, PACKS, 8)),
-            pltpu.SemaphoreType.DMA((2, 8)),
-            pltpu.SemaphoreType.DMA((2, 6)),
+            pltpu.SemaphoreType.DMA((2, 8, 2)),
+            pltpu.SemaphoreType.DMA((2, 6, 2)),
             pltpu.SemaphoreType.DMA((2, 2)),
             pltpu.SemaphoreType.DMA((2, group // 2)),
             pltpu.SemaphoreType.DMA((2, depth)),

time: 99.1 us -> 98.4 us (level)
  no operation moved by 1% of the time
where the time goes in v4:
time: 98.4 us; the launch traced here: 98.3 us
  Pallas kernels  94.5 us (96%)
  local copies, waits for them, and re-layouts  2.52 us (3%)
  between operations  1.29 us (1%)
    pallas_call x1, Pallas kernels, local(): pl.pallas_call(functools.partial(kernel, tiles), out_shape=(jax.ShapeDtyp...  94.5 us
    unnamed x4, local copies, waits for them, and re-layouts  2.52 us

profile of v4, /device:TPU:1, one launch (start us, length us, event | category | flops | bytes accessed | tf_op | source)
XLA Modules:
  0.0 98.3 jit_solution(11710860785771458837)
XLA Ops:
  1.3 94.5 %shard_map.86 = (f32[2,128,256]{2,1,0:T(8,128)}, f32[1024,128]{1,0:T(8,128)}) custom-call(f32[2,128,1024]{2,1,0:T(8,128)} %object_ref.1, f32[1,4,2,128,128]{4,3,2,1,0:T(8,128)} %components_ref.1, f32[4,8]{1,0:T(4,128)} %bitcast.4, f32[8,128,128]{2,1,0:T(8,128)} %amplitudes_ref.1, s32[2,8]{1,0:T(2,128)} %bitcast.5, s32[1]{0:T(128)S(6)} %copy.11.counts_ref, ...), custom_call_target="tpu_custom_call" | custom-call | flops 1610612736 | bytes 4194304 | tf_op jit(solution)/shard_map/pallas_call | solution.py:629
  95.8 0.0 copy-start
  95.8 1.7 %copy.12 = f32[2,128,256]{2,1,0:T(8,128)} copy(f32[2,128,256]{2,1,0:T(8,128)} %get-tuple-element.8) | data formatting | bytes 524288
  97.5 0.0 copy-done
  97.5 0.8 copy.13
Async XLA Ops:
  95.8 1.7 %copy-start = (f32[1024,128]{1,0:T(8,128)S(1)}, f32[1024,128]{1,0:T(8,128)}, u32[]{:S(2)}) copy-start(f32[1024,128]{1,0:T(8,128)} %get-tuple-element.5) | copy-start | bytes 1572868

commit v5 on v4

--- a/solution.py
+++ b/solution.py
@@ -512,11 +512,6 @@
             probe_out.at[at], probe_out.at[at], back_sems.at[:, step], {"tile": beyond(step)}
         )
 
-    for at in range(0, 2):
-        for half, value in whole(at, ()):
-            part[at, half] = value
-            parts[2 * at + half].start()
-
     for copy in spread:
         copy.wait_recv()
     total = half_sum[chunk_rows(chip), :]
@@ -531,7 +526,7 @@
         def _():
             copy.start()
 
-    for at in range(2, 4):
+    for at in range(0, 4):
         for half, value in whole(at, ()):
             part[at, half] = value
             parts[2 * at + half].start()

time: 98.4 us -> 97.6 us (level)
  Pallas kernels: 94.5 us -> 93.5 us
where the time goes in v5:
time: 97.6 us; the launch traced here: 97.4 us
  Pallas kernels  93.5 us (96%)
  local copies, waits for them, and re-layouts  2.52 us (3%)
  between operations  1.29 us (1%)
    pallas_call x1, Pallas kernels, local(): pl.pallas_call(functools.partial(kernel, tiles), out_shape=(jax.ShapeDtyp...  93.5 us
    unnamed x4, local copies, waits for them, and re-layouts  2.52 us

profile of v5, /device:TPU:1, one launch (start us, length us, event | category | flops | bytes accessed | tf_op | source)
XLA Modules:
  0.0 97.4 jit_solution(2100802477657162921)
XLA Ops:
  1.3 93.5 %shard_map.86 = (f32[2,128,256]{2,1,0:T(8,128)}, f32[1024,128]{1,0:T(8,128)}) custom-call(f32[2,128,1024]{2,1,0:T(8,128)} %object_ref.1, f32[1,4,2,128,128]{4,3,2,1,0:T(8,128)} %components_ref.1, f32[4,8]{1,0:T(4,128)} %bitcast.4, f32[8,128,128]{2,1,0:T(8,128)} %amplitudes_ref.1, s32[2,8]{1,0:T(2,128)} %bitcast.5, s32[1]{0:T(128)S(6)} %copy.11.counts_ref, ...), custom_call_target="tpu_custom_call" | custom-call | flops 1610612736 | bytes 4194304 | tf_op jit(solution)/shard_map/pallas_call | solution.py:624
  94.8 0.0 copy-start
  94.8 1.7 %copy.12 = f32[2,128,256]{2,1,0:T(8,128)} copy(f32[2,128,256]{2,1,0:T(8,128)} %get-tuple-element.8) | data formatting | bytes 524288
  96.6 0.0 copy-done
  96.6 0.8 copy.13
Async XLA Ops:
  94.8 1.7 %copy-start = (f32[1024,128]{1,0:T(8,128)S(1)}, f32[1024,128]{1,0:T(8,128)}, u32[]{:S(2)}) copy-start(f32[1024,128]{1,0:T(8,128)} %get-tuple-element.5) | copy-start | bytes 1572868
